TPU v7x, 32 devices: a whole 2x2x4 slice. The times are simulated.
32 devices in a mesh: ctx: 16 (over z, y, x), ch: 2 (over core).
Axes of the slice: x: 2, y: 2, z: 4, core: 2. Of those that a mesh axis runs over, the one named last changes fastest.
Arguments:
- query: bfloat16 [2048, 4096], P('ctx', 'ch'), may hold values from -6 to 6
- key: bfloat16 [2048, 4096], P('ctx', 'ch'), may hold values from -6 to 6
- value: bfloat16 [2048, 4096], P('ctx', 'ch'), may hold values from -6 to 6
- filter_taps: float32 [2048, 256], P('ctx', 'ch'), may hold values from -0.125 to 0.125
- conv_bias: float32 [4096], P('ch'), may hold values from -4 to 4
- norm_gain: float32 [4096], P('ch'), may hold values from 0.1 to 1.9
- pair_list: int32 [136, 3], replicated, may hold values from 0 to 15, as said below
Outputs:
- mixed: bfloat16 [2048, 4096], P('ctx', 'ch')
Inputs may be any that keep to these rules, and one draw needn't show every extreme that they name: `pair_list`: every pair of blocks with source <= target appears once, in no particular order. A row with source = target names the device that holds that block; blocks c and 15 - c are held by two devices whose indices differ only in the lowest bit. Every other pair is executed by one of those two devices for its target block. Each device executes at most 9 pairs.
All inputs are finite; a program needn't handle non-finite values.
Results may differ from a plain program's by a relative error of at most 0.0049.
Values may be sent and summed in bfloat16 or wider, within the bound.
A program may use at most 64 MiB of HBM per device.

v0:
```python
import functools

import jax
import jax.numpy as jnp
from jax import lax
from jax.experimental import pallas as pl
from jax.experimental.pallas import tpu as pltpu
from jax.sharding import PartitionSpec as P

MESH = pl.DeviceIdType.MESH
LANES = 128
STRIP = 8
F32 = jnp.float32
BF16 = jnp.bfloat16


class Plan:
    def __init__(self, mesh, channels, filters, rows):
        self.blocks = mesh.shape["ctx"]
        self.halves = mesh.shape["ch"]
        self.rows = rows
        self.channels = channels
        self.filters = filters
        self.group = channels // filters
        self.each = max(1, filters // self.blocks)
        self.workers = filters // self.each
        self.share = self.each * self.group
        self.parts = 2 if self.each % 2 == 0 else 1
        self.each_part = self.each // self.parts
        self.share_part = self.share // self.parts


def kernel(plan, device_of, holder, query, key, value, taps, bias, gain, out, *scratch):
    blocks, rows, group = plan.blocks, plan.rows, plan.group
    share, part_rows = plan.share, plan.share_part
    parts = range(plan.parts)
    scratch = list(scratch)
    take = lambda count: [scratch.pop(0) for _ in range(count)]
    flipped, taps_flipped, taps_got, toeplitz, total, results, gated, squares = take(8)
    got, ordered, made, staged = (take(plan.parts) for _ in range(4))
    taps_send, taps_recv, square_send, square_recv = take(4)
    go_send, go_recv, back_send, back_recv = (take(plan.parts) for _ in range(4))

    me = lax.axis_index("ctx")
    half = lax.axis_index("ch")

    def only_worker(index):
        if plan.workers == blocks:
            return lambda fn: fn()
        return pl.when(index < plan.workers)

    def peer_of(step):
        return lax.rem(me + step, blocks)

    def taps_copy(peer, slot):
        return pltpu.make_async_remote_copy(
            src_ref=taps_flipped.at[peer],
            dst_ref=taps_got.at[slot],
            send_sem=taps_send.at[peer],
            recv_sem=taps_recv.at[slot],
            device_id={"ctx": peer},
            device_id_type=MESH,
        )

    def go_copy(part, peer, slot):
        first = pl.multiple_of(peer * share + part * part_rows, group)
        return pltpu.make_async_remote_copy(
            src_ref=flipped.at[pl.ds(first, part_rows)],
            dst_ref=got[part].at[slot],
            send_sem=go_send[part].at[peer],
            recv_sem=go_recv[part].at[slot],
            device_id={"ctx": peer},
            device_id_type=MESH,
        )

    def back_copy(part, peer, slot):
        first = pl.multiple_of(slot * share + part * part_rows, group)
        return pltpu.make_async_remote_copy(
            src_ref=staged[part].at[peer],
            dst_ref=results.at[pl.ds(first, part_rows)],
            send_sem=back_send[part].at[peer],
            recv_sem=back_recv[part].at[slot],
            device_id={"ctx": peer},
            device_id_type=MESH,
        )

    def square_copy(peer, slot):
        return pltpu.make_async_remote_copy(
            src_ref=squares.at[half],
            dst_ref=squares.at[slot],
            send_sem=square_send.at[peer],
            recv_sem=square_recv.at[slot],
            device_id={"ch": peer},
            device_id_type=MESH,
        )

    barrier = pltpu.get_barrier_semaphore()

    @pl.loop(1, blocks)
    def _(step):
        pl.semaphore_signal(
            barrier, inc=1, device_id={"ctx": peer_of(step)}, device_id_type=MESH
        )

    for step in range(1, plan.halves):
        pl.semaphore_signal(
            barrier,
            inc=1,
            device_id={"ch": lax.rem(half + step, plan.halves)},
            device_id_type=MESH,
        )

    all_taps = jnp.transpose(taps[...])
    if plan.each == STRIP:
        taps_flipped[...] = all_taps.reshape(plan.workers, STRIP, rows)
    else:
        for worker in range(plan.workers):
            for index in range(plan.each):
                row = worker * plan.each + index
                taps_flipped[worker, index : index + 1, :] = all_taps[row : row + 1, :]

    def signal_tile(columns):
        return key[:, columns].astype(F32) * value[:, columns].astype(F32)

    @pl.loop(0, plan.channels // LANES)
    def _(tile):
        at = pl.ds(pl.multiple_of(tile * LANES, LANES), LANES)
        flipped[at, :] = jnp.transpose(signal_tile(at)).astype(BF16)

    pl.semaphore_wait(barrier, blocks - 1 + plan.halves - 1)

    @pl.loop(1, blocks)
    def _(step):
        peer = peer_of(step)

        @only_worker(peer)
        def _():
            taps_copy(peer, me).start()

    for part in parts:

        @pl.loop(1, blocks)
        def _(step, part=part):
            peer = peer_of(step)

            @only_worker(peer)
            def _():
                go_copy(part, peer, me).start()

    @only_worker(me)
    def _():
        taps_got[me] = taps_flipped[me]
        for part in parts:
            first = pl.multiple_of(me * share + part * part_rows, group)
            got[part][me] = flipped[pl.ds(first, part_rows), :]

        @pl.loop(1, blocks)
        def _(step):
            taps_copy(me, peer_of(step)).wait_recv()

        at_row = lax.broadcasted_iota(jnp.int32, (rows, LANES), 0)
        at_lane = lax.broadcasted_iota(jnp.int32, (rows, LANES), 1)
        ahead = at_lane >= at_row

        @pl.loop(0, plan.each)
        def _(index):
            def one(block, before):
                line = taps_got[block, pl.ds(index, 1), :]
                turned = pltpu.roll(
                    jnp.broadcast_to(line, (rows, LANES)), 0, 1, stride=1, stride_axis=0
                )
                at = pl.ds(pl.multiple_of(block * LANES, LANES), LANES)
                toeplitz[index, :, at] = jnp.where(ahead, turned, before).astype(BF16)
                return turned

            lax.fori_loop(0, blocks, one, jnp.zeros((rows, LANES), F32))

        for part in parts:

            @pl.loop(1, blocks)
            def _(step, part=part):
                go_copy(part, me, peer_of(step)).wait_recv()

            @pl.loop(0, blocks)
            def _(block, part=part):
                piece = got[part][device_of[block]]
                at = pl.ds(pl.multiple_of(block * group, group), group)
                for index in range(plan.each_part):
                    ordered[part][index, at, :] = piece[index * group : (index + 1) * group]

            @pl.loop(0, plan.each_part)
            def _(index, part=part):
                for pair in range(blocks // 2):
                    height = (blocks - 2 * pair) * group
                    product = jnp.dot(
                        ordered[part][index, :height, :],
                        toeplitz[
                            part * plan.each_part + index,
                            :,
                            2 * pair * LANES : 2 * (pair + 1) * LANES,
                        ],
                        preferred_element_type=F32,
                    )
                    even, odd = 2 * pair * group, (2 * pair + 1) * group
                    if pair == 0:
                        total[...] = product[:, :LANES]
                    else:
                        total[even:, :] += product[:, :LANES]
                    total[odd:, :] += product[: height - group, LANES:]
                at = pl.ds(pl.multiple_of(index * group, group), group)
                made[part][:, at, :] = total[...].astype(BF16).reshape(blocks, group, LANES)

            @pl.loop(1, blocks)
            def _(step, part=part):
                peer = peer_of(step)
                staged[part][peer] = made[part][holder[peer]]
                back_copy(part, peer, me).start()

            first = pl.multiple_of(me * share + part * part_rows, group)
            results[pl.ds(first, part_rows), :] = made[part][holder[me]]

    per_tile = LANES // share if share < LANES else 1
    tiles_each = share // LANES if share > LANES else 1

    def finish(tile, sums):
        for near in range(per_tile):
            worker = tile * per_tile + near if tiles_each == 1 else tile // tiles_each

            def wait(worker=worker):
                @pl.when(worker != me)
                def _():
                    for part in parts:
                        back_copy(part, me, worker).wait_recv()

            if tiles_each == 1:
                wait()
            else:
                pl.when(lax.rem(tile, tiles_each) == 0)(wait)
        at = pl.ds(pl.multiple_of(tile * LANES, LANES), LANES)
        conv = jnp.transpose(results[at, :].astype(F32))
        signal = signal_tile(at).astype(BF16).astype(F32)
        product = query[:, at].astype(F32) * (conv + bias[:, at] * signal)
        gated[:, at] = product
        return sums + product * product

    tiles = plan.channels // LANES
    sums = lax.fori_loop(0, tiles, finish, jnp.zeros((rows, LANES), F32))
    squares[half] = jnp.broadcast_to(jnp.sum(sums, axis=1, keepdims=True), (rows, LANES))
    for step in range(1, plan.halves):
        square_copy(lax.rem(half + step, plan.halves), half).start()
    for step in range(1, plan.halves):
        square_copy(half, lax.rem(half + step, plan.halves)).wait_recv()
    whole = squares[0]
    for other in range(1, plan.halves):
        whole = whole + squares[other]
    scaling = lax.rsqrt(whole / (plan.channels * plan.halves) + 1e-05)

    @pl.loop(0, tiles)
    def _(tile):
        at = pl.ds(pl.multiple_of(tile * LANES, LANES), LANES)
        out[:, at] = (gated[:, at] * scaling * gain[:, at]).astype(BF16)

    for step in range(1, plan.halves):
        square_copy(lax.rem(half + step, plan.halves), half).wait_send()

    @pl.loop(1, blocks)
    def _(step):
        peer = peer_of(step)

        @only_worker(peer)
        def _():
            taps_copy(peer, me).wait_send()
            for part in parts:
                go_copy(part, peer, me).wait_send()

        @only_worker(me)
        def _():
            for part in parts:
                back_copy(part, peer, me).wait_send()


def body(mesh, query, key, value, filter_taps, conv_bias, norm_gain, pair_list):
    rows, channels = query.shape
    plan = Plan(mesh, channels, filter_taps.shape[1], rows)
    blocks, parts = plan.blocks, plan.parts
    source, target, runner = pair_list[:, 0], pair_list[:, 1], pair_list[:, 2]
    slots = lax.iota(jnp.int32, blocks)
    on_diag = (source == target)[:, None]
    keeps = on_diag & (source[:, None] == slots[None, :])
    holds = on_diag & (runner[:, None] == slots[None, :])
    device_of = jnp.sum(jnp.where(keeps, runner[:, None], 0), axis=0)
    holder = jnp.sum(jnp.where(holds, source[:, None], 0), axis=0)

    vmem = pl.BlockSpec(memory_space=pltpu.VMEM)
    smem = pl.BlockSpec(memory_space=pltpu.SMEM)
    strip = max(STRIP, plan.each)
    part_piece = (blocks, plan.share_part, LANES)
    sems = pltpu.SemaphoreType.DMA
    scratch = [
        pltpu.VMEM((channels, LANES), BF16),
        pltpu.VMEM((blocks, strip, LANES), F32),
        pltpu.VMEM((blocks, strip, LANES), F32),
        pltpu.VMEM((plan.each, rows, blocks * LANES), BF16),
        pltpu.VMEM((blocks * plan.group, LANES), F32),
        pltpu.VMEM((channels, LANES), BF16),
        pltpu.VMEM((rows, channels), F32),
        pltpu.VMEM((plan.halves, rows, LANES), F32),
    ]
    scratch += [pltpu.VMEM(part_piece, BF16)] * parts
    scratch += [pltpu.VMEM((plan.each_part, blocks * plan.group, LANES), BF16)] * parts
    scratch += [pltpu.VMEM(part_piece, BF16)] * parts
    scratch += [pltpu.VMEM(part_piece, BF16)] * parts
    scratch += [sems((blocks,)), sems((blocks,)), sems((plan.halves,)), sems((plan.halves,))]
    scratch += [sems((blocks,))] * (4 * parts)
    pairs = blocks * (blocks + 2) // 4
    return pl.pallas_call(
        functools.partial(kernel, plan),
        out_shape=jax.ShapeDtypeStruct((rows, channels), BF16),
        in_specs=[smem, smem] + [vmem] * 6,
        out_specs=vmem,
        scratch_shapes=scratch,
        compiler_params=pltpu.CompilerParams(
            collective_id=0, has_side_effects=True, vmem_limit_bytes=48 * 1024 * 1024
        ),
        cost_estimate=pl.CostEstimate(
            flops=2 * plan.each * pairs * plan.group * rows * 2 * LANES,
            bytes_accessed=8 * rows * channels,
            transcendentals=0,
        ),
    )(
        device_of.astype(jnp.int32),
        holder.astype(jnp.int32),
        query,
        key,
        value,
        filter_taps,
        conv_bias[None, :],
        norm_gain[None, :],
    )


def solution(mesh):
    placed = (P("ctx", "ch"), P("ctx", "ch"), P("ctx", "ch"), P("ctx", "ch"), P("ch"), P("ch"), P())
    return jax.shard_map(
        functools.partial(body, mesh),
        mesh=mesh,
        in_specs=placed,
        out_specs=P("ctx", "ch"),
        check_vma=False,
    )
```

profile of v0, /device:TPU:0, one launch (start us, length us, event | category | flops | bytes accessed | tf_op | source)
XLA Modules:
  0.0 45.7 jit_solution(9522793681008857945)
XLA Ops:
  0.0 0.0 copy-start.6
  0.0 0.8 %compare_reduce_fusion = pred[136]{0:T(512)(128)(4,1)S(1)} fusion(s32[136,3]{0,1:T(4,128)} %param.13), kind=kLoop, calls=%fused_computation.6 | loop fusion | flops 136 | bytes 1224 | tf_op jit(solution)/shard_map/eq | solution.py:288
  0.8 0.0 copy-done.6
  0.8 0.0 copy-start.5
  0.8 0.0 copy-start.4
  0.9 0.1 select_reduce_fusion
  1.0 0.5 %copy-done.5 = f32[2048]{0:T(1024)S(1)} copy-done((f32[2048]{0:T(1024)S(1)}, f32[2048]{0:T(1024)}, u32[]{:S(2)}) %copy-start.5) | copy-done | bytes 8216
  1.5 0.0 copy-done.4
  1.5 0.0 copy-start
  1.5 1.0 %copy-done = bf16[128,2048]{1,0:T(8,128)(2,1)S(1)} copy-done((bf16[128,2048]{1,0:T(8,128)(2,1)S(1)}, bf16[128,2048]{1,0:T(8,128)(2,1)}, u32[]{:S(2)}) %copy-start) | copy-done | bytes 524312
  2.6 0.0 copy-start.1
  2.6 1.0 %copy-done.1 = bf16[128,2048]{1,0:T(8,128)(2,1)S(1)} copy-done((bf16[128,2048]{1,0:T(8,128)(2,1)S(1)}, bf16[128,2048]{1,0:T(8,128)(2,1)}, u32[]{:S(2)}) %copy-start.1) | copy-done | bytes 524312
  3.6 0.0 copy-start.2
  3.6 1.0 %copy-done.2 = bf16[128,2048]{1,0:T(8,128)(2,1)S(1)} copy-done((bf16[128,2048]{1,0:T(8,128)(2,1)S(1)}, bf16[128,2048]{1,0:T(8,128)(2,1)}, u32[]{:S(2)}) %copy-start.2) | copy-done | bytes 524312
  4.7 0.0 copy-start.3
  4.7 0.8 %copy-done.3 = f32[128,128]{1,0:T(8,128)S(1)} copy-done((f32[128,128]{1,0:T(8,128)S(1)}, f32[128,128]{1,0:T(8,128)}, u32[]{:S(2)}) %copy-start.3) | copy-done | bytes 65560
  5.5 39.4 %shard_map.73 = bf16[128,2048]{1,0:T(8,128)(2,1)S(1)} custom-call(s32[16]{0:T(128)S(1)} %get-tuple-element.6.device_of, s32[16]{0:T(128)S(1)} %get-tuple-element.5.holder, bf16[128,2048]{1,0:T(8,128)(2,1)S(1)} %copy-done, bf16[128,2048]{1,0:T(8,128)(2,1)S(1)} %copy-done.1, bf16[128,2048]{1,0:T(8,128)(2,1)S(1)} %copy-done.2, f32[128,128]{1,0:T(8,128)S(1)} %copy-done.3, ...), custom_call_target="tpu_custom_call" | custom-call | flops 603979776 | bytes 2097152 | tf_op jit(solution)/shard_map/pallas_call | solution.py:316
  44.9 0.8 %copy.9 = bf16[128,2048]{1,0:T(8,128)(2,1)} copy(bf16[128,2048]{1,0:T(8,128)(2,1)S(1)} %shard_map.73) | data formatting | bytes 1048576
  (1 shorter events, 0.0 us)
Async XLA Ops:
  0.0 0.8 %copy-start.6 = (s32[136,3]{0,1:T(4,128)S(1)}, s32[136,3]{0,1:T(4,128)}, u32[]{:S(2)}) copy-start(s32[136,3]{0,1:T(4,128)} %param.13) | copy-start | bytes 4900
  0.8 0.7 %copy-start.5 = (f32[2048]{0:T(1024)S(1)}, f32[2048]{0:T(1024)}, u32[]{:S(2)}) copy-start(f32[2048]{0:T(1024)} %param.12) | copy-start | bytes 24580
  0.8 0.7 %copy-start.4 = (f32[2048]{0:T(1024)S(1)}, f32[2048]{0:T(1024)}, u32[]{:S(2)}) copy-start(f32[2048]{0:T(1024)} %param.11) | copy-start | bytes 24580
  1.5 1.0 %copy-start = (bf16[128,2048]{1,0:T(8,128)(2,1)S(1)}, bf16[128,2048]{1,0:T(8,128)(2,1)}, u32[]{:S(2)}) copy-start(bf16[128,2048]{1,0:T(8,128)(2,1)} %query.1) | copy-start | bytes 1572868
  2.6 1.0 %copy-start.1 = (bf16[128,2048]{1,0:T(8,128)(2,1)S(1)}, bf16[128,2048]{1,0:T(8,128)(2,1)}, u32[]{:S(2)}) copy-start(bf16[128,2048]{1,0:T(8,128)(2,1)} %key.1) | copy-start | bytes 1572868
  3.6 1.0 %copy-start.2 = (bf16[128,2048]{1,0:T(8,128)(2,1)S(1)}, bf16[128,2048]{1,0:T(8,128)(2,1)}, u32[]{:S(2)}) copy-start(bf16[128,2048]{1,0:T(8,128)(2,1)} %value.1) | copy-start | bytes 1572868
  4.7 0.8 %copy-start.3 = (f32[128,128]{1,0:T(8,128)S(1)}, f32[128,128]{1,0:T(8,128)}, u32[]{:S(2)}) copy-start(f32[128,128]{1,0:T(8,128)} %taps.1) | copy-start | bytes 196612
where the time goes:
time: 46.2 us; the launch traced here: 45.7 us
  Pallas kernels  39.4 us (85%)
  local copies, waits for them, and re-layouts  5.34 us (12%)
  other arithmetic  0.94 us (2%)
    pallas_call x1, Pallas kernels, body(): pl.pallas_call(functools.partial(kernel, plan), out_shape=jax.ShapeDtypeS...  39.4 us
    unnamed x15, local copies, waits for them, and re-layouts  5.34 us

commit v1 on v0

v1 whole, which is shorter than its diff:
```python
import functools

import jax
import jax.numpy as jnp
from jax import lax
from jax.experimental import pallas as pl
from jax.experimental.pallas import tpu as pltpu
from jax.sharding import PartitionSpec as P

MESH = pl.DeviceIdType.MESH
LANES = 128
VMEM_BYTES = 63 * 1024 * 1024
STRIP = 8
F32 = jnp.float32
BF16 = jnp.bfloat16


class Plan:
    def __init__(self, mesh, channels, filters, rows):
        self.blocks = mesh.shape["ctx"]
        self.halves = mesh.shape["ch"]
        self.rows = rows
        self.channels = channels
        self.filters = filters
        self.group = channels // filters
        self.each = max(1, filters // self.blocks)
        self.workers = filters // self.each
        self.share = self.each * self.group
        self.parts = 4 if self.each % 4 == 0 else 1
        self.each_part = self.each // self.parts
        self.share_part = self.share // self.parts
        self.span = channels // self.parts


def kernel(plan, pairs, query, key, value, taps, bias, gated_out, scale, *scratch):
    blocks, rows, group, span = plan.blocks, plan.rows, plan.group, plan.span
    part_rows = plan.share_part
    parts = range(plan.parts)
    scratch = list(scratch)
    take = lambda count: [scratch.pop(0) for _ in range(count)]
    pairs_here, table, table_here, query_here, key_here, value_here, taps_here, bias_here = take(8)
    (gated,) = take(1)
    flipped, taps_rows, taps_flipped, taps_got, toeplitz, total, results, squares = take(8)
    got, ordered, made, staged = (take(plan.parts) for _ in range(4))
    taps_send, taps_recv, square_send, square_recv, loaded, loaded_part = take(6)
    (stored,) = take(1)
    go_send, go_recv, back_send, back_recv = (take(plan.parts) for _ in range(4))

    me = lax.axis_index("ctx")
    half = lax.axis_index("ch")

    def only_worker(index):
        if plan.workers == blocks:
            return lambda fn: fn()
        return pl.when(index < plan.workers)

    def slot_of(step):
        return lax.rem(me + step, blocks)

    bits = [1 << place for place in range((blocks - 1).bit_length())]
    digits = [lax.rem(lax.div(me, bit), 2) for bit in bits]

    def peer_of(mask):
        peer = me
        for bit, digit in zip(bits, digits):
            flip = (mask // bit) % 2 if isinstance(mask, int) else lax.rem(lax.div(mask, bit), 2)
            peer = peer + flip * bit * (1 - 2 * digit)
        return peer

    near = [peer_of(blocks - step) for step in range(1, blocks)] if blocks <= 16 else None

    def each_peer(act):
        if near is not None:
            for peer in near:
                act(peer)
        else:
            pl.loop(1, blocks)(lambda step: act(peer_of(blocks - step)))

    def column_copies(part):
        at = pl.ds(part * span, span)
        return [
            pltpu.make_async_copy(there.at[:, at], here.at[:, at], loaded_part.at[part, place])
            for place, (there, here) in enumerate(((key, key_here), (value, value_here)))
        ]

    def gated_store(part):
        at = pl.ds(part * span, span)
        return pltpu.make_async_copy(gated.at[:, at], gated_out.at[:, at], stored.at[part])

    whole_copies = [
        pltpu.make_async_copy(there, here, loaded.at[place])
        for place, (there, here) in enumerate(
            ((taps, taps_here), (pairs, pairs_here), (bias, bias_here), (query, query_here))
        )
    ]
    taps_load, pairs_load, bias_load, query_load = whole_copies
    table_load = pltpu.make_async_copy(table, table_here, loaded.at[4])

    def taps_copy(peer, slot):
        return pltpu.make_async_remote_copy(
            src_ref=taps_flipped.at[peer],
            dst_ref=taps_got.at[slot],
            send_sem=taps_send.at[peer],
            recv_sem=taps_recv.at[slot],
            device_id={"ctx": peer},
            device_id_type=MESH,
        )

    def go_copy(part, peer, slot):
        first = pl.multiple_of(part * span + peer * part_rows, group)
        return pltpu.make_async_remote_copy(
            src_ref=flipped.at[pl.ds(first, part_rows)],
            dst_ref=got[part].at[slot],
            send_sem=go_send[part].at[peer],
            recv_sem=go_recv[part].at[slot],
            device_id={"ctx": peer},
            device_id_type=MESH,
        )

    def back_copy(part, peer, slot):
        first = pl.multiple_of(part * span + slot * part_rows, group)
        return pltpu.make_async_remote_copy(
            src_ref=staged[part].at[peer],
            dst_ref=results.at[pl.ds(first, part_rows)],
            send_sem=back_send[part].at[peer],
            recv_sem=back_recv[part].at[slot],
            device_id={"ctx": peer},
            device_id_type=MESH,
        )

    def square_copy(peer, slot):
        return pltpu.make_async_remote_copy(
            src_ref=squares.at[half],
            dst_ref=squares.at[slot],
            send_sem=square_send.at[peer],
            recv_sem=square_recv.at[slot],
            device_id={"ch": peer},
            device_id_type=MESH,
        )

    barrier = pltpu.get_barrier_semaphore()

    @each_peer
    def _(peer):
        pl.semaphore_signal(barrier, inc=1, device_id={"ctx": peer}, device_id_type=MESH)

    for step in range(1, plan.halves):
        pl.semaphore_signal(
            barrier,
            inc=1,
            device_id={"ch": lax.rem(half + step, plan.halves)},
            device_id_type=MESH,
        )

    taps_load.start()
    for part in parts:
        for copy in column_copies(part):
            copy.start()
    for copy in (pairs_load, bias_load, query_load):
        copy.start()

    taps_load.wait()
    taps_rows[...] = jnp.transpose(taps_here[...])

    @pl.loop(0, plan.workers)
    def _(worker):
        for part in parts:
            for index in range(plan.each_part):
                row = part * (plan.filters // plan.parts) + worker * plan.each_part + index
                place = part * plan.each_part + index
                taps_flipped[worker, place : place + 1, :] = taps_rows[pl.ds(row, 1), :]

    def signal_tile(columns):
        return key_here[:, columns].astype(F32) * value_here[:, columns].astype(F32)

    part_tiles = span // LANES

    for part in parts:
        for copy in column_copies(part):
            copy.wait()

        @pl.loop(part * part_tiles, (part + 1) * part_tiles)
        def _(tile):
            at = pl.ds(pl.multiple_of(tile * LANES, LANES), LANES)
            flipped[at, :] = jnp.transpose(signal_tile(at)).astype(BF16)

        if part == 0:
            pl.semaphore_wait(barrier, blocks - 1 + plan.halves - 1)

            @each_peer
            def _(peer):
                @only_worker(peer)
                def _():
                    taps_copy(peer, me).start()

        @each_peer
        def _(peer, part=part):
            @only_worker(peer)
            def _():
                go_copy(part, peer, me).start()

    pairs_load.wait()
    source, target, runner = (pairs_here[place : place + 1, :] for place in range(3))
    slots = lax.broadcasted_iota(jnp.int32, (blocks, pairs_here.shape[1]), 0)
    diagonal = source == target
    device_of = jnp.where(diagonal & (source == slots), runner, 0)
    holder = jnp.where(diagonal & (runner == slots), source, 0)
    for place, found in enumerate((device_of, holder)):
        table[place * blocks : (place + 1) * blocks, :] = jnp.broadcast_to(
            jnp.sum(found, axis=1, keepdims=True), (blocks, LANES)
        )
    table_load.start()
    table_load.wait()

    @only_worker(me)
    def _():
        taps_got[me] = taps_flipped[me]
        for part in parts:
            first = pl.multiple_of(part * span + me * part_rows, group)
            got[part][me] = flipped[pl.ds(first, part_rows), :]

        @pl.loop(1, blocks)
        def _(step):
            taps_copy(me, slot_of(step)).wait_recv()

        at_row = lax.broadcasted_iota(jnp.int32, (rows, LANES), 0)
        at_lane = lax.broadcasted_iota(jnp.int32, (rows, LANES), 1)
        ahead = at_lane >= at_row

        for part in parts:

            @pl.loop(part * plan.each_part, (part + 1) * plan.each_part)
            def _(index):
                def one(block, before):
                    line = taps_got[block, pl.ds(index, 1), :]
                    turned = pltpu.roll(
                        jnp.broadcast_to(line, (rows, LANES)), 0, 1, stride=1, stride_axis=0
                    )
                    at = pl.ds(pl.multiple_of(block * LANES, LANES), LANES)
                    toeplitz[index, :, at] = jnp.where(ahead, turned, before).astype(BF16)
                    return turned

                lax.fori_loop(0, blocks, one, jnp.zeros((rows, LANES), F32))

            @pl.loop(1, blocks)
            def _(step, part=part):
                go_copy(part, me, slot_of(step)).wait_recv()

            @pl.loop(0, blocks)
            def _(block, part=part):
                piece = got[part][table_here[block, 0]]
                at = pl.ds(pl.multiple_of(block * group, group), group)
                for index in range(plan.each_part):
                    ordered[part][index, at, :] = piece[index * group : (index + 1) * group]

            @pl.loop(0, plan.each_part)
            def _(index, part=part):
                for pair in range(blocks // 2):
                    height = (blocks - 2 * pair) * group
                    product = jnp.dot(
                        ordered[part][index, :height, :],
                        toeplitz[
                            part * plan.each_part + index,
                            :,
                            2 * pair * LANES : 2 * (pair + 1) * LANES,
                        ],
                        preferred_element_type=F32,
                    )
                    even, odd = 2 * pair * group, (2 * pair + 1) * group
                    if pair == 0:
                        total[...] = product[:, :LANES]
                    else:
                        total[even:, :] += product[:, :LANES]
                    total[odd:, :] += product[: height - group, LANES:]
                at = pl.ds(pl.multiple_of(index * group, group), group)
                made[part][:, at, :] = total[...].astype(BF16).reshape(blocks, group, LANES)

            @each_peer
            def _(peer, part=part):
                staged[part][peer] = made[part][table_here[blocks + peer, 0]]
                back_copy(part, peer, me).start()

            first = pl.multiple_of(part * span + me * part_rows, group)
            results[pl.ds(first, part_rows), :] = made[part][table_here[blocks + me, 0]]

    bias_load.wait()
    query_load.wait()
    per_tile = max(1, LANES // part_rows)
    sums = jnp.zeros((rows, LANES), F32)
    for part in parts:

        def finish(tile, sums, part=part):
            near_tile = tile - part * part_tiles
            for place in range(per_tile):
                worker = lax.div(near_tile * LANES, part_rows) + place

                @pl.when(worker != me)
                def _():
                    back_copy(part, me, worker).wait_recv()

            at = pl.ds(pl.multiple_of(tile * LANES, LANES), LANES)
            conv = jnp.transpose(results[at, :].astype(F32))
            signal = signal_tile(at).astype(BF16).astype(F32)
            product = query_here[:, at].astype(F32) * (conv + bias_here[:, at] * signal)
            gated[:, at] = product
            return sums + product * product

        sums = lax.fori_loop(part * part_tiles, (part + 1) * part_tiles, finish, sums)
        gated_store(part).start()
    squares[half] = jnp.broadcast_to(jnp.sum(sums, axis=1, keepdims=True), (rows, LANES))
    for step in range(1, plan.halves):
        square_copy(lax.rem(half + step, plan.halves), half).start()

    @each_peer
    def _(peer):
        @only_worker(peer)
        def _():
            taps_copy(peer, me).wait_send()
            for part in parts:
                go_copy(part, peer, me).wait_send()

        @only_worker(me)
        def _():
            for part in parts:
                back_copy(part, peer, me).wait_send()

    for step in range(1, plan.halves):
        square_copy(half, lax.rem(half + step, plan.halves)).wait_recv()
    whole = squares[0]
    for other in range(1, plan.halves):
        whole = whole + squares[other]
    scale[...] = lax.rsqrt(whole / (plan.channels * plan.halves) + 1e-05)
    for part in parts:
        gated_store(part).wait()
    for step in range(1, plan.halves):
        square_copy(lax.rem(half + step, plan.halves), half).wait_send()


def body(mesh, query, key, value, filter_taps, conv_bias, norm_gain, pair_list):
    rows, channels = query.shape
    plan = Plan(mesh, channels, filter_taps.shape[1], rows)
    blocks, parts = plan.blocks, plan.parts
    vmem = pl.BlockSpec(memory_space=pltpu.VMEM)
    hbm = pl.BlockSpec(memory_space=pltpu.HBM)
    strip = max(STRIP, plan.each)
    part_piece = (blocks, plan.share_part, LANES)
    sems = pltpu.SemaphoreType.DMA
    scratch = [
        pltpu.VMEM(pair_list.shape[::-1], jnp.int32),
        pltpu.VMEM((2 * blocks, LANES), jnp.int32),
        pltpu.SMEM((2 * blocks, LANES), jnp.int32),
        pltpu.VMEM((rows, channels), BF16),
        pltpu.VMEM((rows, channels), BF16),
        pltpu.VMEM((rows, channels), BF16),
        pltpu.VMEM(filter_taps.shape, F32),
        pltpu.VMEM((1, channels), F32),
        pltpu.VMEM((rows, channels), F32),
        pltpu.VMEM((channels, LANES), BF16),
        pltpu.VMEM((plan.filters, LANES), F32),
        pltpu.VMEM((blocks, strip, LANES), F32),
        pltpu.VMEM((blocks, strip, LANES), F32),
        pltpu.VMEM((plan.each, rows, blocks * LANES), BF16),
        pltpu.VMEM((blocks * plan.group, LANES), F32),
        pltpu.VMEM((channels, LANES), BF16),
        pltpu.VMEM((plan.halves, rows, LANES), F32),
    ]
    scratch += [pltpu.VMEM(part_piece, BF16)] * parts
    scratch += [pltpu.VMEM((plan.each_part, blocks * plan.group, LANES), BF16)] * parts
    scratch += [pltpu.VMEM(part_piece, BF16)] * parts
    scratch += [pltpu.VMEM(part_piece, BF16)] * parts
    scratch += [sems((blocks,)), sems((blocks,)), sems((plan.halves,)), sems((plan.halves,))]
    scratch += [sems((5,)), sems((parts, 2)), sems((parts,))]
    scratch += [sems((blocks,))] * (4 * parts)
    pairs = blocks * (blocks + 2) // 4
    gated, scale = pl.pallas_call(
        functools.partial(kernel, plan),
        out_shape=(
            jax.ShapeDtypeStruct((rows, channels), F32),
            jax.ShapeDtypeStruct((rows, LANES), F32),
        ),
        in_specs=[hbm] * 6,
        out_specs=(hbm, vmem),
        scratch_shapes=scratch,
        compiler_params=pltpu.CompilerParams(
            collective_id=0, has_side_effects=True, vmem_limit_bytes=VMEM_BYTES
        ),
        cost_estimate=pl.CostEstimate(
            flops=2 * plan.each * pairs * plan.group * rows * 2 * LANES,
            bytes_accessed=8 * rows * channels,
            transcendentals=0,
        ),
    )(pair_list.T, query, key, value, filter_taps, conv_bias[None, :])
    return (gated * scale[:, :1] * norm_gain[None, :]).astype(BF16)


def solution(mesh):
    placed = (P("ctx", "ch"), P("ctx", "ch"), P("ctx", "ch"), P("ctx", "ch"), P("ch"), P("ch"), P())
    return jax.shard_map(
        functools.partial(body, mesh),
        mesh=mesh,
        in_specs=placed,
        out_specs=P("ctx", "ch"),
        check_vma=False,
    )
```

time: 46.2 us -> 40.7 us (0.88)
  local copies, waits for them, and re-layouts: 5.34 us -> 0.95 us
  Pallas kernels: 39.4 us -> 37.4 us
  other arithmetic: 0.94 us -> 2.17 us
    unnamed x15 -> x2, local copies, waits for them, and re-layouts: 5.34 us -> 0.01 us
    convert_element_type x0 -> x1, other arithmetic: none -> 2.17 us  [body(): return (gated * scale[:, :1] * norm_gain[None, :]).astype(BF16)]
    pallas_call x1, Pallas kernels: 39.4 us -> 37.4 us  [body(): pl.pallas_call(functools.partial(kernel, plan), out_shape=(jax.ShapeDtype...]
    slice x1, local copies, waits for them, and re-layouts: 0.01 us -> 0.95 us  [body(): return (gated * scale[:, :1] * norm_gain[None, :]).astype(BF16)]
    eq x1 -> x0, other arithmetic: 0.81 us -> none  [body(): on_diag = (source == target)[:, None]]
where the time goes in v1:
time: 40.7 us; the launch traced here: 40.5 us
  Pallas kernels  37.4 us (92%)
  other arithmetic  2.17 us (5%)
  local copies, waits for them, and re-layouts  0.95 us (2%)
    pallas_call x1, Pallas kernels, body(): pl.pallas_call(functools.partial(kernel, plan), out_shape=(jax.ShapeDtype...  37.4 us
    convert_element_type x1, other arithmetic, body(): return (gated * scale[:, :1] * norm_gain[None, :]).astype(BF16)  2.17 us
    slice x1, local copies, waits for them, and re-layouts, body(): return (gated * scale[:, :1] * norm_gain[None, :]).astype(BF16)  0.95 us

profile of v1, /device:TPU:0, one launch (start us, length us, event | category | flops | bytes accessed | tf_op | source)
XLA Modules:
  0.0 40.5 jit_solution(14318067742050909497)
XLA Ops:
  0.0 37.4 %shard_map.73 = (f32[128,2048]{1,0:T(8,128)}, f32[128,128]{1,0:T(8,128)}) custom-call(s32[3,136]{1,0:T(4,128)} %bitcast.3, bf16[128,2048]{1,0:T(8,128)(2,1)} %query.1, bf16[128,2048]{1,0:T(8,128)(2,1)} %key.1, bf16[128,2048]{1,0:T(8,128)(2,1)} %value.1, f32[128,128]{1,0:T(8,128)} %taps.1, f32[1,2048]{1,0:T(1,128)} %bitcast.2), custom_call_target="tpu_custom_call" | custom-call | flops 603979776 | bytes 2097152 | tf_op jit(solution)/shard_map/pallas_call | solution.py:375
  37.4 0.0 copy-start
  37.4 0.9 %slice_reduce_fusion = f32[128]{0:T(128)S(1)} fusion(f32[128,128]{1,0:T(8,128)} %get-tuple-element.8), kind=kLoop, calls=%fused_computation.1 | loop fusion | bytes 1024 | tf_op jit(solution)/shard_map/slice | solution.py:393
  38.3 0.0 copy-done
  38.3 2.2 %multiply_convert_fusion = bf16[128,2048]{1,0:T(8,128)(2,1)} fusion(f32[128,2048]{1,0:T(8,128)} %get-tuple-element.7, f32[2048]{0:T(1024)S(1)} %copy-done, f32[128]{0:T(128)S(1)} %slice_reduce_fusion), kind=kLoop, calls=%fused_computation | loop fusion | flops 786432 | bytes 1581568 | tf_op jit(solution)/shard_map/convert_element_type | solution.py:393
Async XLA Ops:
  37.4 1.0 %copy-start = (f32[2048]{0:T(1024)S(1)}, f32[2048]{0:T(1024)}, u32[]{:S(2)}) copy-start(f32[2048]{0:T(1024)} %param.12) | copy-start | bytes 24580
